TPU v7x, 32 devices: a whole 2x2x4 slice. The times are simulated.
32 devices in a mesh: groups: 2 (over y), rows: 4 (over z), section: 4 (over x, core).
Axes of the slice: x: 2, y: 2, z: 4, core: 2. Of those that a mesh axis runs over, the one named last changes fastest.
Arguments:
- latent: bfloat16 [8, 16, 16, 768], P('groups', 'rows'), parts along dimension 0, may hold values from -1000 to 1000
- target: bfloat16 [8, 16, 16, 768], P('groups', 'rows'), parts along dimension 0, may hold values from -60 to 60
- expand_weight: bfloat16 [4, 768, 1536], P('section', 'rows'), may hold values from -0.21875 to 0.21875
- expand_bias: float32 [4, 1536], P('section'), may hold values from -2 to 2
- reduce_weight: bfloat16 [4, 1536, 768], P('section', 'rows'), may hold values from -0.15625 to 0.15625
- reduce_bias: float32 [4, 768], P('section'), may hold values from -2 to 2
- depth_kernel: float32 [4, 49, 768], P('section'), may hold values from -0.8 to 0.8
- depth_offset: float32 [4, 768], P('section'), may hold values from -2 to 2
- norm_gain: float32 [4, 768], P('section'), may hold values from 0.1 to 1.9
- norm_shift: float32 [4, 768], P('section'), may hold values from -1.2 to 1.2
- layer_scale: float32 [4, 768], P('section'), may hold values from 0.2 to 0.6
Outputs:
- kernel_gradient: float32 [8, 49, 768], P(('groups', 'section')), parts along dimension 0
- offset_gradient: float32 [8, 768], P(('groups', 'section')), parts along dimension 0
- gain_gradient: float32 [8, 768], P(('groups', 'section')), parts along dimension 0
- shift_gradient: float32 [8, 768], P(('groups', 'section')), parts along dimension 0
- scale_gradient: float32 [8, 768], P(('groups', 'section')), parts along dimension 0
There are 2 independent parts, one for each index of `groups`. A program takes and returns all parts, laid end to end along the dimension named above; an argument that names none is the same for every part. Nothing has to cross between parts.
All inputs are finite; a program needn't handle non-finite values.
Results may differ from a plain program's by a relative error of at most 0.005.
The roundings to bfloat16 on the way count: a program that leaves them out, or rounds other values in their place, can miss the bound.
Values may be sent and summed in bfloat16 or wider, within the bound.
A program may use at most 64 MiB of HBM per device.

v0:
```python
import math
import jax
import jax.numpy as jnp
from jax import lax
from jax.sharding import PartitionSpec as P

KS = 7
EPSILON = 1e-06
SQRT_HALF = 0.7071067811865476
INV_ROOT_TAU = 0.3989422804014327


def shifted(value, axis, steps):
    count = lax.axis_size(axis)
    first, last = (max(0, -steps), min(count, count - steps))
    return lax.ppermute(value, axis, [(source, source + steps) for source in range(first, last)])


def with_halo(block, sides, width):
    for axis, dim in sides:
        count = lax.axis_size(axis)
        forward = [(i, i + 1) for i in range(count - 1)]
        backward = [(target, source) for source, target in forward]
        low = lax.ppermute(
            lax.slice_in_dim(block, block.shape[dim] - width, None, axis=dim), axis, forward
        )
        high = lax.ppermute(lax.slice_in_dim(block, 0, width, axis=dim), axis, backward)
        block = jnp.concatenate([low, block, high], axis=dim)
    return block


def depthwise(padded, kernel, offset, height, breadth):
    summed = jnp.zeros((height, breadth, padded.shape[2]), jnp.float32) + offset
    for row_off in range(KS):
        for col_off in range(KS):
            summed = (
                summed
                + kernel[row_off * KS + col_off]
                * padded[row_off : row_off + height, col_off : col_off + breadth]
            )
    return summed


def depthwise_back(padded_slope, kernel, height, breadth):
    margin = KS // 2
    wide_slope = padded_slope.astype(jnp.float32)
    summed = jnp.zeros((height, breadth, padded_slope.shape[2]), jnp.float32)
    for row_off in range(KS):
        for col_off in range(KS):
            first_row = 2 * margin - row_off
            first_col = 2 * margin - col_off
            summed = (
                summed
                + kernel[row_off * KS + col_off]
                * wide_slope[first_row : first_row + height, first_col : first_col + breadth]
            )
    return summed


def kernel_terms(padded, slope, height, breadth):
    pieces = []
    for row_off in range(KS):
        for col_off in range(KS):
            pieces.append(
                jnp.sum(
                    slope * padded[row_off : row_off + height, col_off : col_off + breadth],
                    axis=(0, 1),
                )
            )
    return jnp.stack(pieces)


def normalize(flat):
    centre = jnp.mean(flat, axis=-1, keepdims=True)
    centred = flat - centre
    variance = jnp.mean(centred * centred, axis=-1, keepdims=True)
    inverse = lax.rsqrt(variance + EPSILON)
    return (centred * inverse, inverse)


def gelu_slope(hidden):
    return (
        0.5 * (1.0 + jax.scipy.special.erf(hidden * SQRT_HALF))
        + hidden * jnp.exp(-0.5 * hidden * hidden) * INV_ROOT_TAU
    )


def contract_last(left, right):
    return lax.dot_general(
        left, right, (((1,), (1,)), ((), ())), preferred_element_type=jnp.float32
    )


def project_forward(mixed, gain, shift, w_expand, b_expand, w_reduce, b_reduce):
    normed, inverse = normalize(mixed)
    inputs = (normed * gain + shift).astype(jnp.bfloat16)
    hidden = jnp.dot(inputs, w_expand, preferred_element_type=jnp.float32) + b_expand
    active = jax.nn.gelu(hidden, approximate=False).astype(jnp.bfloat16)
    branch = jnp.dot(active, w_reduce, preferred_element_type=jnp.float32) + b_reduce
    return (normed, inverse, hidden, branch)


def project_backward(incoming, normed, inverse, hidden, branch, gain, scale, w_expand, w_reduce):
    arrived = incoming.astype(jnp.float32)
    scale_term = jnp.sum(arrived * branch, axis=0)
    reduced = (arrived * scale).astype(jnp.bfloat16)
    spread = contract_last(reduced, w_reduce)
    hidden_slope = (spread * gelu_slope(hidden)).astype(jnp.bfloat16)
    normal_slope = contract_last(hidden_slope, w_expand)
    gain_term = jnp.sum(normal_slope * normed, axis=0)
    shift_term = jnp.sum(normal_slope, axis=0)
    scaled = normal_slope * gain
    slope = (
        scaled
        - jnp.mean(scaled, axis=-1, keepdims=True)
        - normed * jnp.mean(scaled * normed, axis=-1, keepdims=True)
    ) * inverse
    offset_term = jnp.sum(slope, axis=0)
    return (slope, scale_term, gain_term, shift_term, offset_term)


def per_device(
    latent,
    target,
    expand_weight,
    expand_bias,
    reduce_weight,
    reduce_bias,
    depth_kernel,
    depth_offset,
    norm_gain,
    norm_shift,
    layer_scale,
):
    sections = lax.axis_size("section")
    section_pos = lax.axis_index("section")
    micro_count, height, breadth, channels = latent.shape
    margin = KS // 2
    moments = micro_count + sections - 1
    total_rows = height * lax.axis_size("rows")
    loss_scale = 1.0 / math.sqrt(micro_count * total_rows * breadth)
    kernel = depth_kernel[0]
    offset = depth_offset[0]
    gain = norm_gain[0]
    shift = norm_shift[0]
    scale = layer_scale[0]
    b_expand = expand_bias[0]
    b_reduce = reduce_bias[0]
    hidden_units = expand_weight.shape[2]
    tokens = height * breadth
    w_expand, w_reduce = (
        lax.all_gather(expand_weight[0], "rows", axis=0, tiled=True),
        lax.all_gather(reduce_weight[0], "rows", axis=0, tiled=True),
    )
    spare_grid = jnp.zeros((height, breadth, channels), jnp.bfloat16)
    kept = (
        jnp.zeros((micro_count, height + 2 * margin, breadth, channels), jnp.bfloat16),
        jnp.zeros((micro_count, tokens, channels), jnp.float32),
        jnp.zeros((micro_count, height, breadth, channels), jnp.bfloat16),
    )
    kept = kept + (
        jnp.zeros((micro_count, tokens, hidden_units), jnp.float32),
        jnp.zeros((micro_count, tokens, channels), jnp.float32),
    )

    def forward_moment(state_in, moment):
        previous, stores = state_in
        arrived = shifted(previous, "section", 1)
        micro_pos = moment - section_pos
        valid = (micro_pos >= 0) & (micro_pos < micro_count)
        safe_pos = jnp.clip(micro_pos, 0, micro_count - 1)
        fresh = lax.dynamic_index_in_dim(latent, safe_pos, 0, keepdims=False)
        source = jnp.where(section_pos == 0, fresh, arrived)
        framed = with_halo(source, (("rows", 0),), margin)

        def forward_working(buffers):
            padded = jnp.pad(framed.astype(jnp.float32), ((0, 0), (margin, margin), (0, 0)))
            mixed = depthwise(padded, kernel, offset, height, breadth).reshape(tokens, channels)
            normed, inverse, hidden, branch = project_forward(
                mixed, gain, shift, w_expand, b_expand, w_reduce, b_reduce
            )
            output = (
                source.astype(jnp.float32) + scale * branch.reshape(height, breadth, channels)
            ).astype(jnp.bfloat16)
            fresh_items = (framed, mixed, output)
            fresh_items = fresh_items + (hidden, branch)
            updated = tuple(
                (
                    lax.dynamic_update_index_in_dim(buffer, element, safe_pos, 0)
                    for buffer, element in zip(buffers, fresh_items)
                )
            )
            return (output, updated)

        def forward_resting(buffers):
            return (spare_grid, buffers)

        output, stores = lax.cond(valid, forward_working, forward_resting, stores)
        return ((output, stores), None)

    forward_state = lax.scan(forward_moment, (spare_grid, kept), jnp.arange(moments))[0]
    kept = forward_state[1]
    back_expand, back_reduce = (
        lax.all_gather(expand_weight[0], "rows", axis=0, tiled=True),
        lax.all_gather(reduce_weight[0], "rows", axis=0, tiled=True),
    )
    zero_sums = (
        jnp.zeros((KS * KS, channels), jnp.float32),
        jnp.zeros((channels,), jnp.float32),
        jnp.zeros((channels,), jnp.float32),
        jnp.zeros((channels,), jnp.float32),
        jnp.zeros((channels,), jnp.float32),
    )

    def backward_moment(state_in, moment):
        previous, totals = state_in
        arrived = shifted(previous, "section", -1)
        micro_pos = moment - (sections - 1 - section_pos)
        valid = (micro_pos >= 0) & (micro_pos < micro_count)
        safe_pos = jnp.clip(micro_pos, 0, micro_count - 1)
        own_output = lax.dynamic_index_in_dim(kept[2], safe_pos, 0, keepdims=False)
        aimed = lax.dynamic_index_in_dim(target, safe_pos, 0, keepdims=False)
        start_slope = (
            (own_output.astype(jnp.float32) - aimed.astype(jnp.float32)) * loss_scale
        ).astype(jnp.bfloat16)
        incoming = jnp.where(section_pos == sections - 1, start_slope, arrived)

        def backward_working(running):
            framed = lax.dynamic_index_in_dim(kept[0], safe_pos, 0, keepdims=False)
            mixed = lax.dynamic_index_in_dim(kept[1], safe_pos, 0, keepdims=False)
            normed, inverse = normalize(mixed)
            hidden = lax.dynamic_index_in_dim(kept[3], safe_pos, 0, keepdims=False)
            branch = lax.dynamic_index_in_dim(kept[4], safe_pos, 0, keepdims=False)
            slope, scale_term, gain_term, shift_term, offset_term = project_backward(
                incoming.reshape(tokens, channels),
                normed,
                inverse,
                hidden,
                branch,
                gain,
                scale,
                back_expand,
                back_reduce,
            )
            padded = jnp.pad(framed.astype(jnp.float32), ((0, 0), (margin, margin), (0, 0)))
            slope_grid = slope.reshape(height, breadth, channels)
            kernel_term = kernel_terms(padded, slope_grid, height, breadth)
            new_totals = (
                running[0] + kernel_term,
                running[1] + offset_term,
                running[2] + gain_term,
                running[3] + shift_term,
                running[4] + scale_term,
            )
            return (slope_grid.astype(jnp.bfloat16), new_totals)

        def backward_resting(running):
            return (spare_grid, running)

        slope_low, totals = lax.cond(valid, backward_working, backward_resting, totals)
        slope_framed = with_halo(slope_low, (("rows", 0),), margin)
        padded_slope = jnp.pad(slope_framed, ((0, 0), (margin, margin), (0, 0)))
        spread_back = depthwise_back(padded_slope, kernel, height, breadth)
        passed = (incoming.astype(jnp.float32) + spread_back).astype(jnp.bfloat16)
        passed = jnp.where(valid, passed, spare_grid)
        return ((passed, totals), None)

    backward_state = lax.scan(backward_moment, (spare_grid, zero_sums), jnp.arange(moments))[0]
    totals = backward_state[1]
    kernel_sum, offset_sum, gain_sum, shift_sum, scale_sum = lax.psum(
        (totals[0], totals[1], totals[2], totals[3], totals[4]), "rows"
    )
    return (kernel_sum[None], offset_sum[None], gain_sum[None], shift_sum[None], scale_sum[None])


def solution(mesh):
    placed = (
        P("groups", "rows", None, None),
        P("groups", "rows", None, None),
        P("section", "rows", None),
        P("section", None),
        P("section", "rows", None),
        P("section", None),
        P("section", None, None),
        P("section", None),
        P("section", None),
        P("section", None),
        P("section", None),
    )
    return jax.shard_map(
        per_device,
        mesh=mesh,
        in_specs=placed,
        out_specs=(
            P(("groups", "section"), None, None),
            P(("groups", "section"), None),
            P(("groups", "section"), None),
            P(("groups", "section"), None),
            P(("groups", "section"), None),
        ),
        check_vma=False,
    )
```

profile of v0, /device:TPU:0, one launch (start us, length us, event | category | flops | bytes accessed | tf_op | source)
XLA Modules:
  0.0 587.9 jit_solution(4347107190480502940)
XLA Ops:
  10.3 52.5 %all-gather.5.cloned.1.call-done = bf16[1,768,1536]{2,1,0:T(8,128)(2,1)} async-done(((bf16[1,192,1536]{2,1,0:T(8,128)(2,1)}), bf16[1,768,1536]{2,1,0:T(8,128)(2,1)}) %all-gather.5.cloned.1.call-update) | async-done | bytes 2359312 | tf_op jit(solution)/shard_map/all_gather | solution.py:152
  62.8 50.9 %all-gather.7.cloned.1.call-done = bf16[1,1536,768]{2,1,0:T(8,128)(2,1)} async-done(((bf16[1,384,768]{2,1,0:T(8,128)(2,1)}), bf16[1,1536,768]{2,1,0:T(8,128)(2,1)}) %all-gather.7.cloned.1.call-update) | async-done | bytes 2359312 | tf_op jit(solution)/shard_map/all_gather | solution.py:153
  120.1 195.3 %while.44 = (s32[]{:T(128)}, bf16[4,16,768]{2,1,0:T(8,128)(2,1)}, bf16[4,10,16,768]{3,2,1,0:T(8,128)(2,1)}, f32[4,64,768]{2,1,0:T(8,128)}, bf16[4,4,16,768]{3,2,...) while((s32[]{:T(128)}, bf16[4,16,768]{2,1,0:T(8,128)(2,1)}, ...), condition=%wide.region_5.6_spmd, body=%wide.region_0.5_spmd.sunk | while | flops 314400832 | bytes 13684738 | solution.py:201
  132.5 20.0 %conditional.5 = (bf16[4,16,768]{2,1,0:T(8,128)(2,1)}, bf16[4,10,16,768]{3,2,1,0:T(8,128)(2,1)}, f32[4,64,768]{2,1,0:T(8,128)}, bf16[4,4,16,768]{3,2,1,0:T(8,128...) conditional(s32[]{:T(128)} %convert_element_type.155, (bf16[4,10,16,768]{3,2,1,0:T(8,128)(2,1)}, ...), branch_computations={%region_1.1_spmd, %region_2.4_spmd} | conditional | flops 314105920 | bytes 11619766 | solution.py:198
  157.9 5.0 collective-permute-start.2
  164.9 20.1 %conditional.5 = (bf16[4,16,768]{2,1,0:T(8,128)(2,1)}, bf16[4,10,16,768]{3,2,1,0:T(8,128)(2,1)}, f32[4,64,768]{2,1,0:T(8,128)}, bf16[4,4,16,768]{3,2,1,0:T(8,128...) conditional(s32[]{:T(128)} %convert_element_type.155, (bf16[4,10,16,768]{3,2,1,0:T(8,128)(2,1)}, ...), branch_computations={%region_1.1_spmd, %region_2.4_spmd} | conditional | flops 314105920 | bytes 11619766 | solution.py:198
  190.3 4.9 collective-permute-start.2
  197.2 20.0 %conditional.5 = (bf16[4,16,768]{2,1,0:T(8,128)(2,1)}, bf16[4,10,16,768]{3,2,1,0:T(8,128)(2,1)}, f32[4,64,768]{2,1,0:T(8,128)}, bf16[4,4,16,768]{3,2,1,0:T(8,128...) conditional(s32[]{:T(128)} %convert_element_type.155, (bf16[4,10,16,768]{3,2,1,0:T(8,128)(2,1)}, ...), branch_computations={%region_1.1_spmd, %region_2.4_spmd} | conditional | flops 314105920 | bytes 11619766 | solution.py:198
  222.6 4.9 collective-permute-start.2
  229.5 20.0 %conditional.5 = (bf16[4,16,768]{2,1,0:T(8,128)(2,1)}, bf16[4,10,16,768]{3,2,1,0:T(8,128)(2,1)}, f32[4,64,768]{2,1,0:T(8,128)}, bf16[4,4,16,768]{3,2,1,0:T(8,128...) conditional(s32[]{:T(128)} %convert_element_type.155, (bf16[4,10,16,768]{3,2,1,0:T(8,128)(2,1)}, ...), branch_computations={%region_1.1_spmd, %region_2.4_spmd} | conditional | flops 314105920 | bytes 11619766 | solution.py:198
  256.9 4.6 collective-permute-start.2
  264.2 24.0 %collective-permute-start = (bf16[4,16,768]{2,1,0:T(8,128)(2,1)}, bf16[4,16,768]{2,1,0:T(8,128)(2,1)S(1)}, u32[]{:S(2)}, u32[]{:S(2)}) collective-permute-start(bf16[4,16,768]{2,1,0:T(8,128)(2,1)} %get-tuple-element.1363), channel_id=1, source_target_pairs={{0,1},{1,2},{2,3},{4,5},{5,6},{6,7},{8,9},{9,10},{10,11},{12,13},{... | collective-permute-start | bytes 294920 | tf_op jit(solution)/shard_map/while/body/eval_jaxpr/ppermute | solution.py:16
  292.2 4.6 collective-permute-start.2
  299.5 4.6 collective-permute-start
  308.2 4.6 collective-permute-start.2
  315.5 227.0 %while.45 = (s32[]{:T(128)}, bf16[4,16,768]{2,1,0:T(8,128)(2,1)S(1)}, f32[49,768]{1,0:T(8,128)S(1)}, f32[768]{0:T(1024)S(1)}, f32[768]{0:T(1024)S(1)}, /*index=5...) while((s32[]{:T(128)}, ...), condition=%wide.region_66.67_spmd.clone, body=%wide.region_6.66_spmd.clone.sunk | while | flops 316624960 | bytes 26198456 | solution.py:268
  321.0 19.3 %collective-permute-done.3 = bf16[4,16,768]{2,1,0:T(8,128)(2,1)S(1)} collective-permute-done((bf16[4,16,768]{2,1,0:T(8,128)(2,1)S(1)}, bf16[4,16,768]{2,1,0:T(8,128)(2,1)S(1)}, u32[]{:S(2)}, u32[]{:S(2)}) %collective-permute-start.3) | collective-permute-done | bytes 98336 | tf_op jit(solution)/shard_map/while/body/eval_jaxpr/ppermute | solution.py:16
  342.7 4.6 collective-permute-start.5
  359.8 4.6 collective-permute-start.5
  373.2 12.3 %collective-permute-done.3 = bf16[4,16,768]{2,1,0:T(8,128)(2,1)S(1)} collective-permute-done((bf16[4,16,768]{2,1,0:T(8,128)(2,1)S(1)}, bf16[4,16,768]{2,1,0:T(8,128)(2,1)S(1)}, u32[]{:S(2)}, u32[]{:S(2)}) %collective-permute-start.3) | collective-permute-done | bytes 98336 | tf_op jit(solution)/shard_map/while/body/eval_jaxpr/ppermute | solution.py:16
  387.9 4.6 collective-permute-start.5
  401.4 33.9 %collective-permute-done.3 = bf16[4,16,768]{2,1,0:T(8,128)(2,1)S(1)} collective-permute-done((bf16[4,16,768]{2,1,0:T(8,128)(2,1)S(1)}, bf16[4,16,768]{2,1,0:T(8,128)(2,1)S(1)}, u32[]{:S(2)}, u32[]{:S(2)}) %collective-permute-start.3) | collective-permute-done | bytes 98336 | tf_op jit(solution)/shard_map/while/body/eval_jaxpr/ppermute | solution.py:16
  436.2 11.6 %conditional.6 = (bf16[4,16,768]{2,1,0:T(8,128)(2,1)S(1)}, f32[49,768]{1,0:T(8,128)S(1)}, f32[768]{0:T(1024)S(1)}, f32[768]{0:T(1024)S(1)}, f32[768]{0:T(1024)S(1)}, /*index=5*/f32[768]{0:T(1024)S(1)}) conditional(s32[]{:T(128)} %convert_element_type.162, (f32[49,768]{1,0:T(8,128)S(1)}, f32[768]{0:T(1024)S(1)}, f32[768]{0:T(1024)S(1)}, ...), branch_computations={%region_7.7_spmd, %region_8.65_spmd} | conditional | flops 309289024 | bytes 13126506 | solution.py:260
  449.2 4.6 collective-permute-start.5
  464.7 11.6 %conditional.6 = (bf16[4,16,768]{2,1,0:T(8,128)(2,1)S(1)}, f32[49,768]{1,0:T(8,128)S(1)}, f32[768]{0:T(1024)S(1)}, f32[768]{0:T(1024)S(1)}, f32[768]{0:T(1024)S(1)}, /*index=5*/f32[768]{0:T(1024)S(1)}) conditional(s32[]{:T(128)} %convert_element_type.162, (f32[49,768]{1,0:T(8,128)S(1)}, f32[768]{0:T(1024)S(1)}, f32[768]{0:T(1024)S(1)}, ...), branch_computations={%region_7.7_spmd, %region_8.65_spmd} | conditional | flops 309289024 | bytes 13126506 | solution.py:260
  477.6 4.6 collective-permute-start.5
  493.3 11.6 %conditional.6 = (bf16[4,16,768]{2,1,0:T(8,128)(2,1)S(1)}, f32[49,768]{1,0:T(8,128)S(1)}, f32[768]{0:T(1024)S(1)}, f32[768]{0:T(1024)S(1)}, f32[768]{0:T(1024)S(1)}, /*index=5*/f32[768]{0:T(1024)S(1)}) conditional(s32[]{:T(128)} %convert_element_type.162, (f32[49,768]{1,0:T(8,128)S(1)}, f32[768]{0:T(1024)S(1)}, f32[768]{0:T(1024)S(1)}, ...), branch_computations={%region_7.7_spmd, %region_8.65_spmd} | conditional | flops 309289024 | bytes 13126506 | solution.py:260
  506.3 4.6 collective-permute-start.5
  521.7 11.6 %conditional.6 = (bf16[4,16,768]{2,1,0:T(8,128)(2,1)S(1)}, f32[49,768]{1,0:T(8,128)S(1)}, f32[768]{0:T(1024)S(1)}, f32[768]{0:T(1024)S(1)}, f32[768]{0:T(1024)S(1)}, /*index=5*/f32[768]{0:T(1024)S(1)}) conditional(s32[]{:T(128)} %convert_element_type.162, (f32[49,768]{1,0:T(8,128)S(1)}, f32[768]{0:T(1024)S(1)}, f32[768]{0:T(1024)S(1)}, ...), branch_computations={%region_7.7_spmd, %region_8.65_spmd} | conditional | flops 309289024 | bytes 13126506 | solution.py:260
  534.6 4.6 collective-permute-start.5
  543.4 21.2 %all-reduce.3 = (f32[1,768]{1,0:T(1,128)}, f32[1,768]{1,0:T(1,128)}, f32[1,768]{1,0:T(1,128)}, f32[1,768]{1,0:T(1,128)}) all-reduce(f32[1,768]{1,0:T(1,128)S(1)} %broadcast_in_dim.73, f32[1,768]{1,0:T(1,128)S(1)} %broadcast_in_dim.74, f32[1,768]{1,0:T(1,128)S(1)} %broadcast_in_dim.75, ...), channel_id=1, replica_groups=mesh['groups'=2,'rows'=4,'section'=4] {'rows'}, use_global_device_ids=true, to_apply=%region_68.69 | all-reduce | flops 3072 | bytes 24576 | tf_op jit(solution)/shard_map/psum | solution.py:270
  564.6 15.2 %all-reduce.6.cloned.1.call-done = f32[1,49,768]{2,0,1:T(1,128)} async-done(((f32[1,49,768]{2,0,1:T(1,128)}), f32[1,49,768]{2,0,1:T(1,128)}) %all-reduce.6.cloned.1.call-update) | async-done | bytes 150544 | tf_op jit(solution)/shard_map/psum | solution.py:270
  (582 shorter events, 269.2 us)
Async XLA Ops:
  7.2 55.6 %all-gather.5.cloned.1.call-start = ((), (), s32[]{:S(2)}) async-start(), calls=%async_computation.1 | async-start | bytes 2949120 | tf_op jit(solution)/shard_map/all_gather | solution.py:152
  7.9 105.8 %all-gather.7.cloned.1.call-start = ((), (), s32[]{:S(2)}) async-start(), calls=%async_computation.2 | async-start | bytes 2949120 | tf_op jit(solution)/shard_map/all_gather | solution.py:153
  8.6 571.1 %all-reduce.6.cloned.1.call-start = ((), (), s32[]{:S(2)}) async-start(), calls=%async_computation | async-start | bytes 301056 | tf_op jit(solution)/shard_map/psum | solution.py:270
  125.9 6.6 %collective-permute-start.2 = (bf16[3,16,768]{2,1,0:T(8,128)(2,1)S(1)}, bf16[3,16,768]{2,1,0:T(8,128)(2,1)S(1)}, u32[]{:S(2)}, u32[]{:S(2)}) collective-permute-start(bf16[3,16,768]{2,1,0:T(8,128)(2,1)S(1)} %get-tuple-element.1229), channel_id=1, source_target_pairs={{0,4},{4,8},{8,12},{1,5},{5,9},{9,13},{2,6},{6,10},{10,14},{3,7},{... | collective-permute-start | bytes 221192 | tf_op jit(solution)/shard_map/while/body/eval_jaxpr/ppermute | solution.py:24
  156.6 6.7 %collective-permute-start.1 = (bf16[3,16,768]{2,1,0:T(8,128)(2,1)S(1)}, bf16[3,16,768]{2,1,0:T(8,128)(2,1)S(1)}, u32[]{:S(2)}, u32[]{:S(2)}) collective-permute-start(bf16[3,16,768]{2,1,0:T(8,128)(2,1)S(1)} %get-tuple-element.1228), channel_id=1, source_target_pairs={{4,0},{8,4},{12,8},{5,1},{9,5},{13,9},{6,2},{10,6},{14,10},{7,3},{... | collective-permute-start | bytes 221192 | tf_op jit(solution)/shard_map/while/body/eval_jaxpr/ppermute | solution.py:27
  157.9 7.0 %collective-permute-start.2 = (bf16[3,16,768]{2,1,0:T(8,128)(2,1)S(1)}, bf16[3,16,768]{2,1,0:T(8,128)(2,1)S(1)}, u32[]{:S(2)}, u32[]{:S(2)}) collective-permute-start(bf16[3,16,768]{2,1,0:T(8,128)(2,1)S(1)} %get-tuple-element.1229), channel_id=1, source_target_pairs={{0,4},{4,8},{8,12},{1,5},{5,9},{9,13},{2,6},{6,10},{10,14},{3,7},{... | collective-permute-start | bytes 221192 | tf_op jit(solution)/shard_map/while/body/eval_jaxpr/ppermute | solution.py:24
  189.0 6.6 %collective-permute-start.1 = (bf16[3,16,768]{2,1,0:T(8,128)(2,1)S(1)}, bf16[3,16,768]{2,1,0:T(8,128)(2,1)S(1)}, u32[]{:S(2)}, u32[]{:S(2)}) collective-permute-start(bf16[3,16,768]{2,1,0:T(8,128)(2,1)S(1)} %get-tuple-element.1228), channel_id=1, source_target_pairs={{4,0},{8,4},{12,8},{5,1},{9,5},{13,9},{6,2},{10,6},{14,10},{7,3},{... | collective-permute-start | bytes 221192 | tf_op jit(solution)/shard_map/while/body/eval_jaxpr/ppermute | solution.py:27
  190.3 6.9 %collective-permute-start.2 = (bf16[3,16,768]{2,1,0:T(8,128)(2,1)S(1)}, bf16[3,16,768]{2,1,0:T(8,128)(2,1)S(1)}, u32[]{:S(2)}, u32[]{:S(2)}) collective-permute-start(bf16[3,16,768]{2,1,0:T(8,128)(2,1)S(1)} %get-tuple-element.1229), channel_id=1, source_target_pairs={{0,4},{4,8},{8,12},{1,5},{5,9},{9,13},{2,6},{6,10},{10,14},{3,7},{... | collective-permute-start | bytes 221192 | tf_op jit(solution)/shard_map/while/body/eval_jaxpr/ppermute | solution.py:24
  221.3 6.6 %collective-permute-start.1 = (bf16[3,16,768]{2,1,0:T(8,128)(2,1)S(1)}, bf16[3,16,768]{2,1,0:T(8,128)(2,1)S(1)}, u32[]{:S(2)}, u32[]{:S(2)}) collective-permute-start(bf16[3,16,768]{2,1,0:T(8,128)(2,1)S(1)} %get-tuple-element.1228), channel_id=1, source_target_pairs={{4,0},{8,4},{12,8},{5,1},{9,5},{13,9},{6,2},{10,6},{14,10},{7,3},{... | collective-permute-start | bytes 221192 | tf_op jit(solution)/shard_map/while/body/eval_jaxpr/ppermute | solution.py:27
  222.6 6.9 %collective-permute-start.2 = (bf16[3,16,768]{2,1,0:T(8,128)(2,1)S(1)}, bf16[3,16,768]{2,1,0:T(8,128)(2,1)S(1)}, u32[]{:S(2)}, u32[]{:S(2)}) collective-permute-start(bf16[3,16,768]{2,1,0:T(8,128)(2,1)S(1)} %get-tuple-element.1229), channel_id=1, source_target_pairs={{0,4},{4,8},{8,12},{1,5},{5,9},{9,13},{2,6},{6,10},{10,14},{3,7},{... | collective-permute-start | bytes 221192 | tf_op jit(solution)/shard_map/while/body/eval_jaxpr/ppermute | solution.py:24
  256.9 6.6 %collective-permute-start.2 = (bf16[3,16,768]{2,1,0:T(8,128)(2,1)S(1)}, bf16[3,16,768]{2,1,0:T(8,128)(2,1)S(1)}, u32[]{:S(2)}, u32[]{:S(2)}) collective-permute-start(bf16[3,16,768]{2,1,0:T(8,128)(2,1)S(1)} %get-tuple-element.1229), channel_id=1, source_target_pairs={{0,4},{4,8},{8,12},{1,5},{5,9},{9,13},{2,6},{6,10},{10,14},{3,7},{... | collective-permute-start | bytes 221192 | tf_op jit(solution)/shard_map/while/body/eval_jaxpr/ppermute | solution.py:24
  264.2 25.8 %collective-permute-start = (bf16[4,16,768]{2,1,0:T(8,128)(2,1)}, bf16[4,16,768]{2,1,0:T(8,128)(2,1)S(1)}, u32[]{:S(2)}, u32[]{:S(2)}) collective-permute-start(bf16[4,16,768]{2,1,0:T(8,128)(2,1)} %get-tuple-element.1363), channel_id=1, source_target_pairs={{0,1},{1,2},{2,3},{4,5},{5,6},{6,7},{8,9},{9,10},{10,11},{12,13},{... | collective-permute-start | bytes 294920 | tf_op jit(solution)/shard_map/while/body/eval_jaxpr/ppermute | solution.py:16
  292.2 6.6 %collective-permute-start.2 = (bf16[3,16,768]{2,1,0:T(8,128)(2,1)S(1)}, bf16[3,16,768]{2,1,0:T(8,128)(2,1)S(1)}, u32[]{:S(2)}, u32[]{:S(2)}) collective-permute-start(bf16[3,16,768]{2,1,0:T(8,128)(2,1)S(1)} %get-tuple-element.1229), channel_id=1, source_target_pairs={{0,4},{4,8},{8,12},{1,5},{5,9},{9,13},{2,6},{6,10},{10,14},{3,7},{... | collective-permute-start | bytes 221192 | tf_op jit(solution)/shard_map/while/body/eval_jaxpr/ppermute | solution.py:24
  308.2 6.6 %collective-permute-start.2 = (bf16[3,16,768]{2,1,0:T(8,128)(2,1)S(1)}, bf16[3,16,768]{2,1,0:T(8,128)(2,1)S(1)}, u32[]{:S(2)}, u32[]{:S(2)}) collective-permute-start(bf16[3,16,768]{2,1,0:T(8,128)(2,1)S(1)} %get-tuple-element.1229), channel_id=1, source_target_pairs={{0,4},{4,8},{8,12},{1,5},{5,9},{9,13},{2,6},{6,10},{10,14},{3,7},{... | collective-permute-start | bytes 221192 | tf_op jit(solution)/shard_map/while/body/eval_jaxpr/ppermute | solution.py:24
  315.5 24.8 %collective-permute-start.3 = (bf16[4,16,768]{2,1,0:T(8,128)(2,1)S(1)}, bf16[4,16,768]{2,1,0:T(8,128)(2,1)S(1)}, u32[]{:S(2)}, u32[]{:S(2)}) collective-permute-start(bf16[4,16,768]{2,1,0:T(8,128)(2,1)S(1)} %broadcast_select_fusion.4), channel_id=1, source_target_pairs={{1,0},{2,1},{3,2},{5,4},{6,5},{7,6},{9,8},{10,9},{11,10},{13,12},{... | collective-permute-start | bytes 294920 | tf_op jit(solution)/shard_map/while/body/eval_jaxpr/ppermute | solution.py:16
  341.4 7.1 %collective-permute-start.4 = (bf16[3,16,768]{2,1,0:T(8,128)(2,1)S(1)}, bf16[3,16,768]{2,1,0:T(8,128)(2,1)S(1)}, u32[]{:S(2)}, u32[]{:S(2)}) collective-permute-start(bf16[3,16,768]{2,1,0:T(8,128)(2,1)S(1)} %get-tuple-element.1258), channel_id=1, source_target_pairs={{4,0},{8,4},{12,8},{5,1},{9,5},{13,9},{6,2},{10,6},{14,10},{7,3},{... | collective-permute-start | bytes 221192 | tf_op jit(solution)/shard_map/while/body/eval_jaxpr/ppermute | solution.py:27
  342.7 6.6 %collective-permute-start.5 = (bf16[3,16,768]{2,1,0:T(8,128)(2,1)S(1)}, bf16[3,16,768]{2,1,0:T(8,128)(2,1)S(1)}, u32[]{:S(2)}, u32[]{:S(2)}) collective-permute-start(bf16[3,16,768]{2,1,0:T(8,128)(2,1)S(1)} %get-tuple-element.1259), channel_id=1, source_target_pairs={{0,4},{4,8},{8,12},{1,5},{5,9},{9,13},{2,6},{6,10},{10,14},{3,7},{... | collective-permute-start | bytes 221192 | tf_op jit(solution)/shard_map/while/body/eval_jaxpr/ppermute | solution.py:24
  350.6 6.8 %collective-permute-start.3 = (bf16[4,16,768]{2,1,0:T(8,128)(2,1)S(1)}, bf16[4,16,768]{2,1,0:T(8,128)(2,1)S(1)}, u32[]{:S(2)}, u32[]{:S(2)}) collective-permute-start(bf16[4,16,768]{2,1,0:T(8,128)(2,1)S(1)} %broadcast_select_fusion.4), channel_id=1, source_target_pairs={{1,0},{2,1},{3,2},{5,4},{6,5},{7,6},{9,8},{10,9},{11,10},{13,12},{... | collective-permute-start | bytes 294920 | tf_op jit(solution)/shard_map/while/body/eval_jaxpr/ppermute | solution.py:16
  358.5 7.1 %collective-permute-start.4 = (bf16[3,16,768]{2,1,0:T(8,128)(2,1)S(1)}, bf16[3,16,768]{2,1,0:T(8,128)(2,1)S(1)}, u32[]{:S(2)}, u32[]{:S(2)}) collective-permute-start(bf16[3,16,768]{2,1,0:T(8,128)(2,1)S(1)} %get-tuple-element.1258), channel_id=1, source_target_pairs={{4,0},{8,4},{12,8},{5,1},{9,5},{13,9},{6,2},{10,6},{14,10},{7,3},{... | collective-permute-start | bytes 221192 | tf_op jit(solution)/shard_map/while/body/eval_jaxpr/ppermute | solution.py:27
  359.8 6.6 %collective-permute-start.5 = (bf16[3,16,768]{2,1,0:T(8,128)(2,1)S(1)}, bf16[3,16,768]{2,1,0:T(8,128)(2,1)S(1)}, u32[]{:S(2)}, u32[]{:S(2)}) collective-permute-start(bf16[3,16,768]{2,1,0:T(8,128)(2,1)S(1)} %get-tuple-element.1259), channel_id=1, source_target_pairs={{0,4},{4,8},{8,12},{1,5},{5,9},{9,13},{2,6},{6,10},{10,14},{3,7},{... | collective-permute-start | bytes 221192 | tf_op jit(solution)/shard_map/while/body/eval_jaxpr/ppermute | solution.py:24
  367.7 17.8 %collective-permute-start.3 = (bf16[4,16,768]{2,1,0:T(8,128)(2,1)S(1)}, bf16[4,16,768]{2,1,0:T(8,128)(2,1)S(1)}, u32[]{:S(2)}, u32[]{:S(2)}) collective-permute-start(bf16[4,16,768]{2,1,0:T(8,128)(2,1)S(1)} %broadcast_select_fusion.4), channel_id=1, source_target_pairs={{1,0},{2,1},{3,2},{5,4},{6,5},{7,6},{9,8},{10,9},{11,10},{13,12},{... | collective-permute-start | bytes 294920 | tf_op jit(solution)/shard_map/while/body/eval_jaxpr/ppermute | solution.py:16
  386.6 7.1 %collective-permute-start.4 = (bf16[3,16,768]{2,1,0:T(8,128)(2,1)S(1)}, bf16[3,16,768]{2,1,0:T(8,128)(2,1)S(1)}, u32[]{:S(2)}, u32[]{:S(2)}) collective-permute-start(bf16[3,16,768]{2,1,0:T(8,128)(2,1)S(1)} %get-tuple-element.1258), channel_id=1, source_target_pairs={{4,0},{8,4},{12,8},{5,1},{9,5},{13,9},{6,2},{10,6},{14,10},{7,3},{... | collective-permute-start | bytes 221192 | tf_op jit(solution)/shard_map/while/body/eval_jaxpr/ppermute | solution.py:27
  387.9 6.6 %collective-permute-start.5 = (bf16[3,16,768]{2,1,0:T(8,128)(2,1)S(1)}, bf16[3,16,768]{2,1,0:T(8,128)(2,1)S(1)}, u32[]{:S(2)}, u32[]{:S(2)}) collective-permute-start(bf16[3,16,768]{2,1,0:T(8,128)(2,1)S(1)} %get-tuple-element.1259), channel_id=1, source_target_pairs={{0,4},{4,8},{8,12},{1,5},{5,9},{9,13},{2,6},{6,10},{10,14},{3,7},{... | collective-permute-start | bytes 221192 | tf_op jit(solution)/shard_map/while/body/eval_jaxpr/ppermute | solution.py:24
  395.9 39.4 %collective-permute-start.3 = (bf16[4,16,768]{2,1,0:T(8,128)(2,1)S(1)}, bf16[4,16,768]{2,1,0:T(8,128)(2,1)S(1)}, u32[]{:S(2)}, u32[]{:S(2)}) collective-permute-start(bf16[4,16,768]{2,1,0:T(8,128)(2,1)S(1)} %broadcast_select_fusion.4), channel_id=1, source_target_pairs={{1,0},{2,1},{3,2},{5,4},{6,5},{7,6},{9,8},{10,9},{11,10},{13,12},{... | collective-permute-start | bytes 294920 | tf_op jit(solution)/shard_map/while/body/eval_jaxpr/ppermute | solution.py:16
  447.9 7.1 %collective-permute-start.4 = (bf16[3,16,768]{2,1,0:T(8,128)(2,1)S(1)}, bf16[3,16,768]{2,1,0:T(8,128)(2,1)S(1)}, u32[]{:S(2)}, u32[]{:S(2)}) collective-permute-start(bf16[3,16,768]{2,1,0:T(8,128)(2,1)S(1)} %get-tuple-element.1258), channel_id=1, source_target_pairs={{4,0},{8,4},{12,8},{5,1},{9,5},{13,9},{6,2},{10,6},{14,10},{7,3},{... | collective-permute-start | bytes 221192 | tf_op jit(solution)/shard_map/while/body/eval_jaxpr/ppermute | solution.py:27
  449.2 6.6 %collective-permute-start.5 = (bf16[3,16,768]{2,1,0:T(8,128)(2,1)S(1)}, bf16[3,16,768]{2,1,0:T(8,128)(2,1)S(1)}, u32[]{:S(2)}, u32[]{:S(2)}) collective-permute-start(bf16[3,16,768]{2,1,0:T(8,128)(2,1)S(1)} %get-tuple-element.1259), channel_id=1, source_target_pairs={{0,4},{4,8},{8,12},{1,5},{5,9},{9,13},{2,6},{6,10},{10,14},{3,7},{... | collective-permute-start | bytes 221192 | tf_op jit(solution)/shard_map/while/body/eval_jaxpr/ppermute | solution.py:24
  476.3 7.1 %collective-permute-start.4 = (bf16[3,16,768]{2,1,0:T(8,128)(2,1)S(1)}, bf16[3,16,768]{2,1,0:T(8,128)(2,1)S(1)}, u32[]{:S(2)}, u32[]{:S(2)}) collective-permute-start(bf16[3,16,768]{2,1,0:T(8,128)(2,1)S(1)} %get-tuple-element.1258), channel_id=1, source_target_pairs={{4,0},{8,4},{12,8},{5,1},{9,5},{13,9},{6,2},{10,6},{14,10},{7,3},{... | collective-permute-start | bytes 221192 | tf_op jit(solution)/shard_map/while/body/eval_jaxpr/ppermute | solution.py:27
  485.6 6.7 %collective-permute-start.3 = (bf16[4,16,768]{2,1,0:T(8,128)(2,1)S(1)}, bf16[4,16,768]{2,1,0:T(8,128)(2,1)S(1)}, u32[]{:S(2)}, u32[]{:S(2)}) collective-permute-start(bf16[4,16,768]{2,1,0:T(8,128)(2,1)S(1)} %broadcast_select_fusion.4), channel_id=1, source_target_pairs={{1,0},{2,1},{3,2},{5,4},{6,5},{7,6},{9,8},{10,9},{11,10},{13,12},{... | collective-permute-start | bytes 294920 | tf_op jit(solution)/shard_map/while/body/eval_jaxpr/ppermute | solution.py:16
  505.0 7.1 %collective-permute-start.4 = (bf16[3,16,768]{2,1,0:T(8,128)(2,1)S(1)}, bf16[3,16,768]{2,1,0:T(8,128)(2,1)S(1)}, u32[]{:S(2)}, u32[]{:S(2)}) collective-permute-start(bf16[3,16,768]{2,1,0:T(8,128)(2,1)S(1)} %get-tuple-element.1258), channel_id=1, source_target_pairs={{4,0},{8,4},{12,8},{5,1},{9,5},{13,9},{6,2},{10,6},{14,10},{7,3},{... | collective-permute-start | bytes 221192 | tf_op jit(solution)/shard_map/while/body/eval_jaxpr/ppermute | solution.py:27
  506.3 6.6 %collective-permute-start.5 = (bf16[3,16,768]{2,1,0:T(8,128)(2,1)S(1)}, bf16[3,16,768]{2,1,0:T(8,128)(2,1)S(1)}, u32[]{:S(2)}, u32[]{:S(2)}) collective-permute-start(bf16[3,16,768]{2,1,0:T(8,128)(2,1)S(1)} %get-tuple-element.1259), channel_id=1, source_target_pairs={{0,4},{4,8},{8,12},{1,5},{5,9},{9,13},{2,6},{6,10},{10,14},{3,7},{... | collective-permute-start | bytes 221192 | tf_op jit(solution)/shard_map/while/body/eval_jaxpr/ppermute | solution.py:24
  533.3 7.1 %collective-permute-start.4 = (bf16[3,16,768]{2,1,0:T(8,128)(2,1)S(1)}, bf16[3,16,768]{2,1,0:T(8,128)(2,1)S(1)}, u32[]{:S(2)}, u32[]{:S(2)}) collective-permute-start(bf16[3,16,768]{2,1,0:T(8,128)(2,1)S(1)} %get-tuple-element.1258), channel_id=1, source_target_pairs={{4,0},{8,4},{12,8},{5,1},{9,5},{13,9},{6,2},{10,6},{14,10},{7,3},{... | collective-permute-start | bytes 221192 | tf_op jit(solution)/shard_map/while/body/eval_jaxpr/ppermute | solution.py:27
  534.6 6.6 %collective-permute-start.5 = (bf16[3,16,768]{2,1,0:T(8,128)(2,1)S(1)}, bf16[3,16,768]{2,1,0:T(8,128)(2,1)S(1)}, u32[]{:S(2)}, u32[]{:S(2)}) collective-permute-start(bf16[3,16,768]{2,1,0:T(8,128)(2,1)S(1)} %get-tuple-element.1259), channel_id=1, source_target_pairs={{0,4},{4,8},{8,12},{1,5},{5,9},{9,13},{2,6},{6,10},{10,14},{3,7},{... | collective-permute-start | bytes 221192 | tf_op jit(solution)/shard_map/while/body/eval_jaxpr/ppermute | solution.py:24
  (22 other events, 156.7 us)
Sparse Core Ops, SparseCore 0:
  9.6 53.1 all-gather.4
  64.4 49.2 all-gather.6
  543.4 36.2 all-reduce.5
where the time goes:
time: 595 us; the launch traced here: 588 us
  waiting for transfers between devices  209 us (35%)
  starting transfers between devices  130 us (22%)
  local copies, waits for them, and re-layouts  86.1 us (14%)
  other arithmetic  81.1 us (14%)
  matrix products  33.8 us (6%)
  blocking collectives  21.2 us (4%)
  between operations  13.8 us (2%)
  loops' own time  12.3 us (2%)
    ppermute x14, waiting for transfers between devices, shifted(): lax.ppermute(value, axis, [(source, source + steps) for source in range(f...  70.1 us
    ppermute x14, starting transfers between devices, with_halo(): lax.ppermute(lax.slice_in_dim(block, block.shape[dim] - width, None, axis...  65.5 us
    all_gather x1, waiting for transfers between devices, per_device(): lax.all_gather(expand_weight[0], 'rows', axis=0, tiled=True)  52.5 us
    all_gather x1, waiting for transfers between devices, per_device(): lax.all_gather(reduce_weight[0], 'rows', axis=0, tiled=True)  50.9 us
    ppermute x14, starting transfers between devices, shifted(): lax.ppermute(value, axis, [(source, source + steps) for source in range(f...  46.5 us
    slice x21, local copies, waits for them, and re-layouts, depthwise_back(): kernel[row_off * KS + col_off]  28.6 us
    slice x12, local copies, waits for them, and re-layouts, depthwise(): kernel[row_off * KS + col_off]  23.8 us
    psum x1, blocking collectives, per_device(): lax.psum((totals[0], totals[1], totals[2], totals[3], totals[4]), 'rows')  21.2 us
  transfers between devices with their start and end apart: 45, of which 31 were waited for; matrix products, arithmetic and copies ran while one was open for 7% of the time, Pallas kernels for 0%

commit v1 on v0

--- a/solution.py
+++ b/solution.py
@@ -8,6 +8,25 @@
 EPSILON = 1e-06
 SQRT_HALF = 0.7071067811865476
 INV_ROOT_TAU = 0.3989422804014327
+
+
+def gather_around(x, axis, dim):
+    size, index, rows = (lax.axis_size(axis), lax.axis_index(axis), x.shape[dim])
+    right = [(i, (i + 1) % size) for i in range(size)]
+    behind = [(i, (i - 1) % size) for i in range(size)]
+    out = jnp.zeros((*x.shape[:dim], size * rows, *x.shape[dim + 1 :]), x.dtype)
+    out = lax.dynamic_update_slice_in_dim(out, x, index * rows, axis=dim)
+    from_left = from_right = x
+    middle = size // 2
+    for lap in range(1, middle + 1):
+        from_left = lax.ppermute(from_left, axis, right)
+        out = lax.dynamic_update_slice_in_dim(out, from_left, (index - lap) % size * rows, axis=dim)
+        if lap < size - middle:
+            from_right = lax.ppermute(from_right, axis, behind)
+            out = lax.dynamic_update_slice_in_dim(
+                out, from_right, (index + lap) % size * rows, axis=dim
+            )
+    return out
 
 
 def shifted(value, axis, steps):
@@ -150,7 +169,7 @@
     tokens = height * breadth
     w_expand, w_reduce = (
         lax.all_gather(expand_weight[0], "rows", axis=0, tiled=True),
-        lax.all_gather(reduce_weight[0], "rows", axis=0, tiled=True),
+        gather_around(reduce_weight[0], "rows", 0),
     )
     spare_grid = jnp.zeros((height, breadth, channels), jnp.bfloat16)
     kept = (

time: 595 us -> 574 us (0.965)
  waiting for transfers between devices: 209 us -> 168 us
  starting transfers between devices: 130 us -> 146 us
    ppermute x0 -> x3, waiting for transfers between devices: none -> 52.6 us  [the longest x1 29.3 us: gather_around(): from_right = lax.ppermute(from_right, axis, behind)]
    all_gather x1, waiting for transfers between devices: 50.9 us -> 0.01 us  [per_device(): lax.all_gather(reduce_weight[0], 'rows', axis=0, tiled=True)]
    all_gather x1, waiting for transfers between devices: 52.5 us -> 7.66 us  [per_device(): lax.all_gather(expand_weight[0], 'rows', axis=0, tiled=True)]
    ppermute x0 -> x3, starting transfers between devices: none -> 15.4 us  [the longest x2 13.3 us: gather_around(): from_left = lax.ppermute(from_left, axis, right)]
  transfers between devices with their start and end apart: 45 -> 48, of which waited for: 31 -> 32; matrix products, arithmetic and copies ran while one was open for 7% -> 25% of each run, Pallas kernels for 0% -> 0%
where the time goes in v1:
time: 574 us; the launch traced here: 567 us
  waiting for transfers between devices  168 us (29%)
  starting transfers between devices  146 us (25%)
  local copies, waits for them, and re-layouts  90.1 us (16%)
  other arithmetic  81.1 us (14%)
  matrix products  33.8 us (6%)
  blocking collectives  21.3 us (4%)
  between operations  13.9 us (2%)
  loops' own time  12.2 us (2%)
    ppermute x14, waiting for transfers between devices, shifted(): lax.ppermute(value, axis, [(source, source + steps) for source in range(f...  70.5 us
    ppermute x14, starting transfers between devices, with_halo(): lax.ppermute(lax.slice_in_dim(block, block.shape[dim] - width, None, axis...  65.2 us
    ppermute x14, starting transfers between devices, shifted(): lax.ppermute(value, axis, [(source, source + steps) for source in range(f...  47 us
    ppermute x1, waiting for transfers between devices, gather_around(): from_right = lax.ppermute(from_right, axis, behind)  29.3 us
    slice x21, local copies, waits for them, and re-layouts, depthwise_back(): kernel[row_off * KS + col_off]  27.9 us
    slice x12, local copies, waits for them, and re-layouts, depthwise(): kernel[row_off * KS + col_off]  23.6 us
    ppermute x2, waiting for transfers between devices, gather_around(): from_left = lax.ppermute(from_left, axis, right)  23.3 us
    psum x1, blocking collectives, per_device(): lax.psum((totals[0], totals[1], totals[2], totals[3], totals[4]), 'rows')  21.3 us
  transfers between devices with their start and end apart: 48, of which 32 were waited for; matrix products, arithmetic and copies ran while one was open for 25% of the time, Pallas kernels for 0%

profile of v1, /device:TPU:0, one launch (start us, length us, event | category | flops | bytes accessed | tf_op | source)
XLA Modules:
  0.0 566.6 jit_solution(15437609279000571600)
XLA Ops:
  13.1 17.2 %collective-permute-done.6 = bf16[384,768]{1,0:T(8,128)(2,1)} collective-permute-done((bf16[384,768]{1,0:T(8,128)(2,1)}, bf16[384,768]{1,0:T(8,128)(2,1)}, u32[]{:S(2)}, u32[]{:S(2)}) %collective-permute-start.6) | collective-permute-done | bytes 589856 | tf_op jit(solution)/shard_map/ppermute | solution.py:22
  30.3 10.2 %collective-permute-start.8 = (bf16[384,768]{1,0:T(8,128)(2,1)}, bf16[384,768]{1,0:T(8,128)(2,1)}, u32[]{:S(2)}, u32[]{:S(2)}) collective-permute-start(bf16[384,768]{1,0:T(8,128)(2,1)} %collective-permute-done.6), channel_id=1, source_target_pairs={{0,4},{4,8},{8,12},{12,0},{1,5},{5,9},{9,13},{13,1},{2,6},{6,10},{... | collective-permute-start | bytes 1769480 | tf_op jit(solution)/shard_map/ppermute | solution.py:22
  43.5 29.3 %collective-permute-done.7 = bf16[384,768]{1,0:T(8,128)(2,1)} collective-permute-done((bf16[384,768]{1,0:T(8,128)(2,1)}, bf16[384,768]{1,0:T(8,128)(2,1)}, u32[]{:S(2)}, u32[]{:S(2)}) %collective-permute-start.7) | collective-permute-done | bytes 589856 | tf_op jit(solution)/shard_map/ppermute | solution.py:25
  73.9 6.2 %collective-permute-done.8 = bf16[384,768]{1,0:T(8,128)(2,1)} collective-permute-done((bf16[384,768]{1,0:T(8,128)(2,1)}, bf16[384,768]{1,0:T(8,128)(2,1)}, u32[]{:S(2)}, u32[]{:S(2)}) %collective-permute-start.8) | collective-permute-done | bytes 589856 | tf_op jit(solution)/shard_map/ppermute | solution.py:22
  82.6 7.7 %all-gather.5.cloned.1.call-done = bf16[1,768,1536]{2,1,0:T(8,128)(2,1)} async-done(((bf16[1,192,1536]{2,1,0:T(8,128)(2,1)}), bf16[1,768,1536]{2,1,0:T(8,128)(2,1)}) %all-gather.5.cloned.1.call-update) | async-done | bytes 2359312 | tf_op jit(solution)/shard_map/all_gather | solution.py:171
  96.6 197.6 %while.44 = (s32[]{:T(128)}, bf16[4,16,768]{2,1,0:T(8,128)(2,1)}, bf16[4,10,16,768]{3,2,1,0:T(8,128)(2,1)}, f32[4,64,768]{2,1,0:T(8,128)}, bf16[4,4,16,768]{3,2,...) while((s32[]{:T(128)}, bf16[4,16,768]{2,1,0:T(8,128)(2,1)}, ...), condition=%wide.region_5.6_spmd, body=%wide.region_0.5_spmd.sunk | while | flops 314400832 | bytes 13684738 | solution.py:220
  111.6 20.0 %conditional.5 = (bf16[4,16,768]{2,1,0:T(8,128)(2,1)}, bf16[4,10,16,768]{3,2,1,0:T(8,128)(2,1)}, f32[4,64,768]{2,1,0:T(8,128)}, bf16[4,4,16,768]{3,2,1,0:T(8,128...) conditional(s32[]{:T(128)} %convert_element_type.155, (bf16[4,10,16,768]{3,2,1,0:T(8,128)(2,1)}, ...), branch_computations={%region_1.1_spmd, %region_2.4_spmd} | conditional | flops 314105920 | bytes 11619766 | solution.py:217
  136.9 4.7 collective-permute-start.2
  143.6 20.0 %conditional.5 = (bf16[4,16,768]{2,1,0:T(8,128)(2,1)}, bf16[4,10,16,768]{3,2,1,0:T(8,128)(2,1)}, f32[4,64,768]{2,1,0:T(8,128)}, bf16[4,4,16,768]{3,2,1,0:T(8,128...) conditional(s32[]{:T(128)} %convert_element_type.155, (bf16[4,10,16,768]{3,2,1,0:T(8,128)(2,1)}, ...), branch_computations={%region_1.1_spmd, %region_2.4_spmd} | conditional | flops 314105920 | bytes 11619766 | solution.py:217
  168.9 5.0 collective-permute-start.2
  175.8 20.0 %conditional.5 = (bf16[4,16,768]{2,1,0:T(8,128)(2,1)}, bf16[4,10,16,768]{3,2,1,0:T(8,128)(2,1)}, f32[4,64,768]{2,1,0:T(8,128)}, bf16[4,4,16,768]{3,2,1,0:T(8,128...) conditional(s32[]{:T(128)} %convert_element_type.155, (bf16[4,10,16,768]{3,2,1,0:T(8,128)(2,1)}, ...), branch_computations={%region_1.1_spmd, %region_2.4_spmd} | conditional | flops 314105920 | bytes 11619766 | solution.py:217
  201.1 4.9 collective-permute-start.2
  208.0 20.0 %conditional.5 = (bf16[4,16,768]{2,1,0:T(8,128)(2,1)}, bf16[4,10,16,768]{3,2,1,0:T(8,128)(2,1)}, f32[4,64,768]{2,1,0:T(8,128)}, bf16[4,4,16,768]{3,2,1,0:T(8,128...) conditional(s32[]{:T(128)} %convert_element_type.155, (bf16[4,10,16,768]{3,2,1,0:T(8,128)(2,1)}, ...), branch_computations={%region_1.1_spmd, %region_2.4_spmd} | conditional | flops 314105920 | bytes 11619766 | solution.py:217
  235.7 4.6 collective-permute-start.2
  243.0 24.0 %collective-permute-start = (bf16[4,16,768]{2,1,0:T(8,128)(2,1)}, bf16[4,16,768]{2,1,0:T(8,128)(2,1)S(1)}, u32[]{:S(2)}, u32[]{:S(2)}) collective-permute-start(bf16[4,16,768]{2,1,0:T(8,128)(2,1)} %get-tuple-element.1363), channel_id=1, source_target_pairs={{0,1},{1,2},{2,3},{4,5},{5,6},{6,7},{8,9},{9,10},{10,11},{12,13},{... | collective-permute-start | bytes 294920 | tf_op jit(solution)/shard_map/while/body/eval_jaxpr/ppermute | solution.py:35
  271.0 4.6 collective-permute-start.2
  286.9 4.6 collective-permute-start.2
  294.2 226.8 %while.45 = (s32[]{:T(128)}, bf16[4,16,768]{2,1,0:T(8,128)(2,1)S(1)}, f32[49,768]{1,0:T(8,128)S(1)}, f32[768]{0:T(1024)S(1)}, f32[768]{0:T(1024)S(1)}, /*index=5...) while((s32[]{:T(128)}, ...), condition=%wide.region_66.67_spmd.clone, body=%wide.region_6.66_spmd.clone.sunk | while | flops 316624960 | bytes 26198456 | solution.py:287
  299.7 19.4 %collective-permute-done.3 = bf16[4,16,768]{2,1,0:T(8,128)(2,1)S(1)} collective-permute-done((bf16[4,16,768]{2,1,0:T(8,128)(2,1)S(1)}, bf16[4,16,768]{2,1,0:T(8,128)(2,1)S(1)}, u32[]{:S(2)}, u32[]{:S(2)}) %collective-permute-start.3) | collective-permute-done | bytes 98336 | tf_op jit(solution)/shard_map/while/body/eval_jaxpr/ppermute | solution.py:35
  321.4 4.6 collective-permute-start.5
  338.5 4.6 collective-permute-start.5
  351.9 12.4 %collective-permute-done.3 = bf16[4,16,768]{2,1,0:T(8,128)(2,1)S(1)} collective-permute-done((bf16[4,16,768]{2,1,0:T(8,128)(2,1)S(1)}, bf16[4,16,768]{2,1,0:T(8,128)(2,1)S(1)}, u32[]{:S(2)}, u32[]{:S(2)}) %collective-permute-start.3) | collective-permute-done | bytes 98336 | tf_op jit(solution)/shard_map/while/body/eval_jaxpr/ppermute | solution.py:35
  366.7 4.6 collective-permute-start.5
  380.1 33.9 %collective-permute-done.3 = bf16[4,16,768]{2,1,0:T(8,128)(2,1)S(1)} collective-permute-done((bf16[4,16,768]{2,1,0:T(8,128)(2,1)S(1)}, bf16[4,16,768]{2,1,0:T(8,128)(2,1)S(1)}, u32[]{:S(2)}, u32[]{:S(2)}) %collective-permute-start.3) | collective-permute-done | bytes 98336 | tf_op jit(solution)/shard_map/while/body/eval_jaxpr/ppermute | solution.py:35
  414.9 11.6 %conditional.6 = (bf16[4,16,768]{2,1,0:T(8,128)(2,1)S(1)}, f32[49,768]{1,0:T(8,128)S(1)}, f32[768]{0:T(1024)S(1)}, f32[768]{0:T(1024)S(1)}, f32[768]{0:T(1024)S(1)}, /*index=5*/f32[768]{0:T(1024)S(1)}) conditional(s32[]{:T(128)} %convert_element_type.162, (f32[49,768]{1,0:T(8,128)S(1)}, f32[768]{0:T(1024)S(1)}, f32[768]{0:T(1024)S(1)}, ...), branch_computations={%region_7.7_spmd, %region_8.65_spmd} | conditional | flops 309289024 | bytes 13126506 | solution.py:279
  427.9 4.6 collective-permute-start.5
  443.4 11.6 %conditional.6 = (bf16[4,16,768]{2,1,0:T(8,128)(2,1)S(1)}, f32[49,768]{1,0:T(8,128)S(1)}, f32[768]{0:T(1024)S(1)}, f32[768]{0:T(1024)S(1)}, f32[768]{0:T(1024)S(1)}, /*index=5*/f32[768]{0:T(1024)S(1)}) conditional(s32[]{:T(128)} %convert_element_type.162, (f32[49,768]{1,0:T(8,128)S(1)}, f32[768]{0:T(1024)S(1)}, f32[768]{0:T(1024)S(1)}, ...), branch_computations={%region_7.7_spmd, %region_8.65_spmd} | conditional | flops 309289024 | bytes 13126506 | solution.py:279
  456.4 4.6 collective-permute-start.5
  472.0 11.6 %conditional.6 = (bf16[4,16,768]{2,1,0:T(8,128)(2,1)S(1)}, f32[49,768]{1,0:T(8,128)S(1)}, f32[768]{0:T(1024)S(1)}, f32[768]{0:T(1024)S(1)}, f32[768]{0:T(1024)S(1)}, /*index=5*/f32[768]{0:T(1024)S(1)}) conditional(s32[]{:T(128)} %convert_element_type.162, (f32[49,768]{1,0:T(8,128)S(1)}, f32[768]{0:T(1024)S(1)}, f32[768]{0:T(1024)S(1)}, ...), branch_computations={%region_7.7_spmd, %region_8.65_spmd} | conditional | flops 309289024 | bytes 13126506 | solution.py:279
  500.2 11.6 %conditional.6 = (bf16[4,16,768]{2,1,0:T(8,128)(2,1)S(1)}, f32[49,768]{1,0:T(8,128)S(1)}, f32[768]{0:T(1024)S(1)}, f32[768]{0:T(1024)S(1)}, f32[768]{0:T(1024)S(1)}, /*index=5*/f32[768]{0:T(1024)S(1)}) conditional(s32[]{:T(128)} %convert_element_type.162, (f32[49,768]{1,0:T(8,128)S(1)}, f32[768]{0:T(1024)S(1)}, f32[768]{0:T(1024)S(1)}, ...), branch_computations={%region_7.7_spmd, %region_8.65_spmd} | conditional | flops 309289024 | bytes 13126506 | solution.py:279
  521.9 21.3 %all-reduce.3 = (f32[1,768]{1,0:T(1,128)}, f32[1,768]{1,0:T(1,128)}, f32[1,768]{1,0:T(1,128)}, f32[1,768]{1,0:T(1,128)}) all-reduce(f32[1,768]{1,0:T(1,128)S(1)} %broadcast_in_dim.77, f32[1,768]{1,0:T(1,128)S(1)} %broadcast_in_dim.78, f32[1,768]{1,0:T(1,128)S(1)} %broadcast_in_dim.79, ...), channel_id=1, replica_groups=mesh['groups'=2,'rows'=4,'section'=4] {'rows'}, use_global_device_ids=true, to_apply=%region_68.69 | all-reduce | flops 3072 | bytes 24576 | tf_op jit(solution)/shard_map/psum | solution.py:289
  543.2 15.2 %all-reduce.6.cloned.1.call-done = f32[1,49,768]{2,0,1:T(1,128)} async-done(((f32[1,49,768]{2,0,1:T(1,128)}), f32[1,49,768]{2,0,1:T(1,128)}) %all-reduce.6.cloned.1.call-update) | async-done | bytes 150544 | tf_op jit(solution)/shard_map/psum | solution.py:289
  (597 shorter events, 294.4 us)
Async XLA Ops:
  7.2 83.0 %all-gather.5.cloned.1.call-start = ((), (), s32[]{:S(2)}) async-start(), calls=%async_computation.1 | async-start | bytes 2949120 | tf_op jit(solution)/shard_map/all_gather | solution.py:171
  7.9 286.3 %all-gather.7.cloned.1.call-start = ((), (), s32[]{:S(2)}) async-start(), calls=%async_computation.2 | async-start | bytes 2949120 | tf_op jit(solution)/shard_map/all_gather | solution.py:224
  8.0 22.3 %collective-permute-start.6 = (bf16[384,768]{1,0:T(8,128)(2,1)}, bf16[384,768]{1,0:T(8,128)(2,1)}, u32[]{:S(2)}, u32[]{:S(2)}) collective-permute-start(bf16[384,768]{1,0:T(8,128)(2,1)} %bitcast.185), channel_id=1, source_target_pairs={{0,4},{4,8},{8,12},{12,0},{1,5},{5,9},{9,13},{13,1},{2,6},{6,10},{... | collective-permute-start | bytes 1769480 | tf_op jit(solution)/shard_map/ppermute | solution.py:22
  11.0 61.8 %collective-permute-start.7 = (bf16[384,768]{1,0:T(8,128)(2,1)}, bf16[384,768]{1,0:T(8,128)(2,1)}, u32[]{:S(2)}, u32[]{:S(2)}) collective-permute-start(bf16[384,768]{1,0:T(8,128)(2,1)} %bitcast.186), channel_id=1, source_target_pairs={{0,12},{4,0},{8,4},{12,8},{1,13},{5,1},{9,5},{13,9},{2,14},{6,2},{... | collective-permute-start | bytes 1769480 | tf_op jit(solution)/shard_map/ppermute | solution.py:25
  30.3 49.8 %collective-permute-start.8 = (bf16[384,768]{1,0:T(8,128)(2,1)}, bf16[384,768]{1,0:T(8,128)(2,1)}, u32[]{:S(2)}, u32[]{:S(2)}) collective-permute-start(bf16[384,768]{1,0:T(8,128)(2,1)} %collective-permute-done.6), channel_id=1, source_target_pairs={{0,4},{4,8},{8,12},{12,0},{1,5},{5,9},{9,13},{13,1},{2,6},{6,10},{... | collective-permute-start | bytes 1769480 | tf_op jit(solution)/shard_map/ppermute | solution.py:22
  40.5 518.0 %all-reduce.6.cloned.1.call-start = ((), (), s32[]{:S(2)}) async-start(), calls=%async_computation | async-start | bytes 301056 | tf_op jit(solution)/shard_map/psum | solution.py:289
  101.3 10.2 %collective-permute-start.1 = (bf16[3,16,768]{2,1,0:T(8,128)(2,1)S(1)}, bf16[3,16,768]{2,1,0:T(8,128)(2,1)S(1)}, u32[]{:S(2)}, u32[]{:S(2)}) collective-permute-start(bf16[3,16,768]{2,1,0:T(8,128)(2,1)S(1)} %get-tuple-element.1228), channel_id=1, source_target_pairs={{4,0},{8,4},{12,8},{5,1},{9,5},{13,9},{6,2},{10,6},{14,10},{7,3},{... | collective-permute-start | bytes 221192 | tf_op jit(solution)/shard_map/while/body/eval_jaxpr/ppermute | solution.py:46
  102.6 8.9 %collective-permute-start.2 = (bf16[3,16,768]{2,1,0:T(8,128)(2,1)S(1)}, bf16[3,16,768]{2,1,0:T(8,128)(2,1)S(1)}, u32[]{:S(2)}, u32[]{:S(2)}) collective-permute-start(bf16[3,16,768]{2,1,0:T(8,128)(2,1)S(1)} %get-tuple-element.1229), channel_id=1, source_target_pairs={{0,4},{4,8},{8,12},{1,5},{5,9},{9,13},{2,6},{6,10},{10,14},{3,7},{... | collective-permute-start | bytes 221192 | tf_op jit(solution)/shard_map/while/body/eval_jaxpr/ppermute | solution.py:43
  135.6 6.6 %collective-permute-start.1 = (bf16[3,16,768]{2,1,0:T(8,128)(2,1)S(1)}, bf16[3,16,768]{2,1,0:T(8,128)(2,1)S(1)}, u32[]{:S(2)}, u32[]{:S(2)}) collective-permute-start(bf16[3,16,768]{2,1,0:T(8,128)(2,1)S(1)} %get-tuple-element.1228), channel_id=1, source_target_pairs={{4,0},{8,4},{12,8},{5,1},{9,5},{13,9},{6,2},{10,6},{14,10},{7,3},{... | collective-permute-start | bytes 221192 | tf_op jit(solution)/shard_map/while/body/eval_jaxpr/ppermute | solution.py:46
  136.9 6.7 %collective-permute-start.2 = (bf16[3,16,768]{2,1,0:T(8,128)(2,1)S(1)}, bf16[3,16,768]{2,1,0:T(8,128)(2,1)S(1)}, u32[]{:S(2)}, u32[]{:S(2)}) collective-permute-start(bf16[3,16,768]{2,1,0:T(8,128)(2,1)S(1)} %get-tuple-element.1229), channel_id=1, source_target_pairs={{0,4},{4,8},{8,12},{1,5},{5,9},{9,13},{2,6},{6,10},{10,14},{3,7},{... | collective-permute-start | bytes 221192 | tf_op jit(solution)/shard_map/while/body/eval_jaxpr/ppermute | solution.py:43
  167.6 6.6 %collective-permute-start.1 = (bf16[3,16,768]{2,1,0:T(8,128)(2,1)S(1)}, bf16[3,16,768]{2,1,0:T(8,128)(2,1)S(1)}, u32[]{:S(2)}, u32[]{:S(2)}) collective-permute-start(bf16[3,16,768]{2,1,0:T(8,128)(2,1)S(1)} %get-tuple-element.1228), channel_id=1, source_target_pairs={{4,0},{8,4},{12,8},{5,1},{9,5},{13,9},{6,2},{10,6},{14,10},{7,3},{... | collective-permute-start | bytes 221192 | tf_op jit(solution)/shard_map/while/body/eval_jaxpr/ppermute | solution.py:46
  168.9 6.9 %collective-permute-start.2 = (bf16[3,16,768]{2,1,0:T(8,128)(2,1)S(1)}, bf16[3,16,768]{2,1,0:T(8,128)(2,1)S(1)}, u32[]{:S(2)}, u32[]{:S(2)}) collective-permute-start(bf16[3,16,768]{2,1,0:T(8,128)(2,1)S(1)} %get-tuple-element.1229), channel_id=1, source_target_pairs={{0,4},{4,8},{8,12},{1,5},{5,9},{9,13},{2,6},{6,10},{10,14},{3,7},{... | collective-permute-start | bytes 221192 | tf_op jit(solution)/shard_map/while/body/eval_jaxpr/ppermute | solution.py:43
  199.8 6.6 %collective-permute-start.1 = (bf16[3,16,768]{2,1,0:T(8,128)(2,1)S(1)}, bf16[3,16,768]{2,1,0:T(8,128)(2,1)S(1)}, u32[]{:S(2)}, u32[]{:S(2)}) collective-permute-start(bf16[3,16,768]{2,1,0:T(8,128)(2,1)S(1)} %get-tuple-element.1228), channel_id=1, source_target_pairs={{4,0},{8,4},{12,8},{5,1},{9,5},{13,9},{6,2},{10,6},{14,10},{7,3},{... | collective-permute-start | bytes 221192 | tf_op jit(solution)/shard_map/while/body/eval_jaxpr/ppermute | solution.py:46
  201.1 6.9 %collective-permute-start.2 = (bf16[3,16,768]{2,1,0:T(8,128)(2,1)S(1)}, bf16[3,16,768]{2,1,0:T(8,128)(2,1)S(1)}, u32[]{:S(2)}, u32[]{:S(2)}) collective-permute-start(bf16[3,16,768]{2,1,0:T(8,128)(2,1)S(1)} %get-tuple-element.1229), channel_id=1, source_target_pairs={{0,4},{4,8},{8,12},{1,5},{5,9},{9,13},{2,6},{6,10},{10,14},{3,7},{... | collective-permute-start | bytes 221192 | tf_op jit(solution)/shard_map/while/body/eval_jaxpr/ppermute | solution.py:43
  235.7 6.6 %collective-permute-start.2 = (bf16[3,16,768]{2,1,0:T(8,128)(2,1)S(1)}, bf16[3,16,768]{2,1,0:T(8,128)(2,1)S(1)}, u32[]{:S(2)}, u32[]{:S(2)}) collective-permute-start(bf16[3,16,768]{2,1,0:T(8,128)(2,1)S(1)} %get-tuple-element.1229), channel_id=1, source_target_pairs={{0,4},{4,8},{8,12},{1,5},{5,9},{9,13},{2,6},{6,10},{10,14},{3,7},{... | collective-permute-start | bytes 221192 | tf_op jit(solution)/shard_map/while/body/eval_jaxpr/ppermute | solution.py:43
  243.0 25.8 %collective-permute-start = (bf16[4,16,768]{2,1,0:T(8,128)(2,1)}, bf16[4,16,768]{2,1,0:T(8,128)(2,1)S(1)}, u32[]{:S(2)}, u32[]{:S(2)}) collective-permute-start(bf16[4,16,768]{2,1,0:T(8,128)(2,1)} %get-tuple-element.1363), channel_id=1, source_target_pairs={{0,1},{1,2},{2,3},{4,5},{5,6},{6,7},{8,9},{9,10},{10,11},{12,13},{... | collective-permute-start | bytes 294920 | tf_op jit(solution)/shard_map/while/body/eval_jaxpr/ppermute | solution.py:35
  286.9 6.6 %collective-permute-start.2 = (bf16[3,16,768]{2,1,0:T(8,128)(2,1)S(1)}, bf16[3,16,768]{2,1,0:T(8,128)(2,1)S(1)}, u32[]{:S(2)}, u32[]{:S(2)}) collective-permute-start(bf16[3,16,768]{2,1,0:T(8,128)(2,1)S(1)} %get-tuple-element.1229), channel_id=1, source_target_pairs={{0,4},{4,8},{8,12},{1,5},{5,9},{9,13},{2,6},{6,10},{10,14},{3,7},{... | collective-permute-start | bytes 221192 | tf_op jit(solution)/shard_map/while/body/eval_jaxpr/ppermute | solution.py:43
  294.3 24.8 %collective-permute-start.3 = (bf16[4,16,768]{2,1,0:T(8,128)(2,1)S(1)}, bf16[4,16,768]{2,1,0:T(8,128)(2,1)S(1)}, u32[]{:S(2)}, u32[]{:S(2)}) collective-permute-start(bf16[4,16,768]{2,1,0:T(8,128)(2,1)S(1)} %broadcast_select_fusion.4), channel_id=1, source_target_pairs={{1,0},{2,1},{3,2},{5,4},{6,5},{7,6},{9,8},{10,9},{11,10},{13,12},{... | collective-permute-start | bytes 294920 | tf_op jit(solution)/shard_map/while/body/eval_jaxpr/ppermute | solution.py:35
  320.1 7.1 %collective-permute-start.4 = (bf16[3,16,768]{2,1,0:T(8,128)(2,1)S(1)}, bf16[3,16,768]{2,1,0:T(8,128)(2,1)S(1)}, u32[]{:S(2)}, u32[]{:S(2)}) collective-permute-start(bf16[3,16,768]{2,1,0:T(8,128)(2,1)S(1)} %get-tuple-element.1258), channel_id=1, source_target_pairs={{4,0},{8,4},{12,8},{5,1},{9,5},{13,9},{6,2},{10,6},{14,10},{7,3},{... | collective-permute-start | bytes 221192 | tf_op jit(solution)/shard_map/while/body/eval_jaxpr/ppermute | solution.py:46
  321.4 6.6 %collective-permute-start.5 = (bf16[3,16,768]{2,1,0:T(8,128)(2,1)S(1)}, bf16[3,16,768]{2,1,0:T(8,128)(2,1)S(1)}, u32[]{:S(2)}, u32[]{:S(2)}) collective-permute-start(bf16[3,16,768]{2,1,0:T(8,128)(2,1)S(1)} %get-tuple-element.1259), channel_id=1, source_target_pairs={{0,4},{4,8},{8,12},{1,5},{5,9},{9,13},{2,6},{6,10},{10,14},{3,7},{... | collective-permute-start | bytes 221192 | tf_op jit(solution)/shard_map/while/body/eval_jaxpr/ppermute | solution.py:43
  329.4 6.8 %collective-permute-start.3 = (bf16[4,16,768]{2,1,0:T(8,128)(2,1)S(1)}, bf16[4,16,768]{2,1,0:T(8,128)(2,1)S(1)}, u32[]{:S(2)}, u32[]{:S(2)}) collective-permute-start(bf16[4,16,768]{2,1,0:T(8,128)(2,1)S(1)} %broadcast_select_fusion.4), channel_id=1, source_target_pairs={{1,0},{2,1},{3,2},{5,4},{6,5},{7,6},{9,8},{10,9},{11,10},{13,12},{... | collective-permute-start | bytes 294920 | tf_op jit(solution)/shard_map/while/body/eval_jaxpr/ppermute | solution.py:35
  337.2 7.1 %collective-permute-start.4 = (bf16[3,16,768]{2,1,0:T(8,128)(2,1)S(1)}, bf16[3,16,768]{2,1,0:T(8,128)(2,1)S(1)}, u32[]{:S(2)}, u32[]{:S(2)}) collective-permute-start(bf16[3,16,768]{2,1,0:T(8,128)(2,1)S(1)} %get-tuple-element.1258), channel_id=1, source_target_pairs={{4,0},{8,4},{12,8},{5,1},{9,5},{13,9},{6,2},{10,6},{14,10},{7,3},{... | collective-permute-start | bytes 221192 | tf_op jit(solution)/shard_map/while/body/eval_jaxpr/ppermute | solution.py:46
  338.5 6.6 %collective-permute-start.5 = (bf16[3,16,768]{2,1,0:T(8,128)(2,1)S(1)}, bf16[3,16,768]{2,1,0:T(8,128)(2,1)S(1)}, u32[]{:S(2)}, u32[]{:S(2)}) collective-permute-start(bf16[3,16,768]{2,1,0:T(8,128)(2,1)S(1)} %get-tuple-element.1259), channel_id=1, source_target_pairs={{0,4},{4,8},{8,12},{1,5},{5,9},{9,13},{2,6},{6,10},{10,14},{3,7},{... | collective-permute-start | bytes 221192 | tf_op jit(solution)/shard_map/while/body/eval_jaxpr/ppermute | solution.py:43
  346.5 17.8 %collective-permute-start.3 = (bf16[4,16,768]{2,1,0:T(8,128)(2,1)S(1)}, bf16[4,16,768]{2,1,0:T(8,128)(2,1)S(1)}, u32[]{:S(2)}, u32[]{:S(2)}) collective-permute-start(bf16[4,16,768]{2,1,0:T(8,128)(2,1)S(1)} %broadcast_select_fusion.4), channel_id=1, source_target_pairs={{1,0},{2,1},{3,2},{5,4},{6,5},{7,6},{9,8},{10,9},{11,10},{13,12},{... | collective-permute-start | bytes 294920 | tf_op jit(solution)/shard_map/while/body/eval_jaxpr/ppermute | solution.py:35
  365.4 7.1 %collective-permute-start.4 = (bf16[3,16,768]{2,1,0:T(8,128)(2,1)S(1)}, bf16[3,16,768]{2,1,0:T(8,128)(2,1)S(1)}, u32[]{:S(2)}, u32[]{:S(2)}) collective-permute-start(bf16[3,16,768]{2,1,0:T(8,128)(2,1)S(1)} %get-tuple-element.1258), channel_id=1, source_target_pairs={{4,0},{8,4},{12,8},{5,1},{9,5},{13,9},{6,2},{10,6},{14,10},{7,3},{... | collective-permute-start | bytes 221192 | tf_op jit(solution)/shard_map/while/body/eval_jaxpr/ppermute | solution.py:46
  374.7 39.3 %collective-permute-start.3 = (bf16[4,16,768]{2,1,0:T(8,128)(2,1)S(1)}, bf16[4,16,768]{2,1,0:T(8,128)(2,1)S(1)}, u32[]{:S(2)}, u32[]{:S(2)}) collective-permute-start(bf16[4,16,768]{2,1,0:T(8,128)(2,1)S(1)} %broadcast_select_fusion.4), channel_id=1, source_target_pairs={{1,0},{2,1},{3,2},{5,4},{6,5},{7,6},{9,8},{10,9},{11,10},{13,12},{... | collective-permute-start | bytes 294920 | tf_op jit(solution)/shard_map/while/body/eval_jaxpr/ppermute | solution.py:35
  426.6 7.1 %collective-permute-start.4 = (bf16[3,16,768]{2,1,0:T(8,128)(2,1)S(1)}, bf16[3,16,768]{2,1,0:T(8,128)(2,1)S(1)}, u32[]{:S(2)}, u32[]{:S(2)}) collective-permute-start(bf16[3,16,768]{2,1,0:T(8,128)(2,1)S(1)} %get-tuple-element.1258), channel_id=1, source_target_pairs={{4,0},{8,4},{12,8},{5,1},{9,5},{13,9},{6,2},{10,6},{14,10},{7,3},{... | collective-permute-start | bytes 221192 | tf_op jit(solution)/shard_map/while/body/eval_jaxpr/ppermute | solution.py:46
  435.8 6.6 %collective-permute-start.3 = (bf16[4,16,768]{2,1,0:T(8,128)(2,1)S(1)}, bf16[4,16,768]{2,1,0:T(8,128)(2,1)S(1)}, u32[]{:S(2)}, u32[]{:S(2)}) collective-permute-start(bf16[4,16,768]{2,1,0:T(8,128)(2,1)S(1)} %broadcast_select_fusion.4), channel_id=1, source_target_pairs={{1,0},{2,1},{3,2},{5,4},{6,5},{7,6},{9,8},{10,9},{11,10},{13,12},{... | collective-permute-start | bytes 294920 | tf_op jit(solution)/shard_map/while/body/eval_jaxpr/ppermute | solution.py:35
  455.1 7.1 %collective-permute-start.4 = (bf16[3,16,768]{2,1,0:T(8,128)(2,1)S(1)}, bf16[3,16,768]{2,1,0:T(8,128)(2,1)S(1)}, u32[]{:S(2)}, u32[]{:S(2)}) collective-permute-start(bf16[3,16,768]{2,1,0:T(8,128)(2,1)S(1)} %get-tuple-element.1258), channel_id=1, source_target_pairs={{4,0},{8,4},{12,8},{5,1},{9,5},{13,9},{6,2},{10,6},{14,10},{7,3},{... | collective-permute-start | bytes 221192 | tf_op jit(solution)/shard_map/while/body/eval_jaxpr/ppermute | solution.py:46
  464.3 6.7 %collective-permute-start.3 = (bf16[4,16,768]{2,1,0:T(8,128)(2,1)S(1)}, bf16[4,16,768]{2,1,0:T(8,128)(2,1)S(1)}, u32[]{:S(2)}, u32[]{:S(2)}) collective-permute-start(bf16[4,16,768]{2,1,0:T(8,128)(2,1)S(1)} %broadcast_select_fusion.4), channel_id=1, source_target_pairs={{1,0},{2,1},{3,2},{5,4},{6,5},{7,6},{9,8},{10,9},{11,10},{13,12},{... | collective-permute-start | bytes 294920 | tf_op jit(solution)/shard_map/while/body/eval_jaxpr/ppermute | solution.py:35
  483.6 7.1 %collective-permute-start.4 = (bf16[3,16,768]{2,1,0:T(8,128)(2,1)S(1)}, bf16[3,16,768]{2,1,0:T(8,128)(2,1)S(1)}, u32[]{:S(2)}, u32[]{:S(2)}) collective-permute-start(bf16[3,16,768]{2,1,0:T(8,128)(2,1)S(1)} %get-tuple-element.1258), channel_id=1, source_target_pairs={{4,0},{8,4},{12,8},{5,1},{9,5},{13,9},{6,2},{10,6},{14,10},{7,3},{... | collective-permute-start | bytes 221192 | tf_op jit(solution)/shard_map/while/body/eval_jaxpr/ppermute | solution.py:46
  511.8 7.1 %collective-permute-start.4 = (bf16[3,16,768]{2,1,0:T(8,128)(2,1)S(1)}, bf16[3,16,768]{2,1,0:T(8,128)(2,1)S(1)}, u32[]{:S(2)}, u32[]{:S(2)}) collective-permute-start(bf16[3,16,768]{2,1,0:T(8,128)(2,1)S(1)} %get-tuple-element.1258), channel_id=1, source_target_pairs={{4,0},{8,4},{12,8},{5,1},{9,5},{13,9},{6,2},{10,6},{14,10},{7,3},{... | collective-permute-start | bytes 221192 | tf_op jit(solution)/shard_map/while/body/eval_jaxpr/ppermute | solution.py:46
  (27 other events, 162.7 us)
Sparse Core Ops, SparseCore 0:
  9.6 80.5 all-gather.4
  91.8 51.8 all-gather.6
  522.0 36.4 all-reduce.5
